TPU v7x, 128 devices: a whole 4x4x4 slice. The times are simulated.
128 devices in a mesh: rep: 16 (over x, z), tp: 8 (over y, core).
Axes of the slice: x: 4, y: 4, z: 4, core: 2. Of those that a mesh axis runs over, the one named last changes fastest.
Arguments:
- inputs: bfloat16 [16384, 1024], P(('rep', 'tp')), may hold values from -6 to 6
- cotangent: bfloat16 [16384, 1024], P(('rep', 'tp')), may hold values from -0.29882812 to 0.29882812
- weight_in: bfloat16 [2, 1024, 4, 8, 128], P(None, None, None, 'tp'), may hold values from -0.1875 to 0.1875
- weight_out: bfloat16 [2, 8, 128, 1024], P(None, 'tp'), may hold values from -0.1875 to 0.1875
- bias_table: float32 [2, 8, 16], P(None, 'tp'), may hold values from -4 to 4
- lengths: int32 [16], P('rep'), may hold values from 256 to 1024, as said below
- stamps: int32 [16, 1024], P('rep'), may hold values from 0 to 111, as said below
- factor_in: float32 [2, 8, 32, 512], P(None, 'tp'), may hold values from -6 to 6
- factor_out: float32 [2, 8, 32, 1024], P(None, 'tp'), may hold values from -6 to 6
- error_in: float32 [16, 2, 8, 1024, 512], P('rep', None, 'tp'), may hold values from -3 to 3
- error_out: float32 [16, 2, 8, 128, 1024], P('rep', None, 'tp'), may hold values from -3 to 3
Outputs:
- update_in: float32 [2, 8, 1024, 512], P(None, 'tp')
- update_out: float32 [2, 8, 128, 1024], P(None, 'tp')
- factor_in_next: float32 [2, 8, 32, 512], P(None, 'tp')
- factor_out_next: float32 [2, 8, 32, 1024], P(None, 'tp')
- error_in_next: float32 [16, 2, 8, 1024, 512], P('rep', None, 'tp')
- error_out_next: float32 [16, 2, 8, 128, 1024], P('rep', None, 'tp')
Inputs may be any that keep to these rules, and one draw needn't show every extreme that they name: `lengths`: A sequence's events are its first length positions; some sequence has exactly 1024. `stamps`: non-decreasing along each sequence; within a sequence the stamps rise by at most 48 from the first to the last event.
All inputs are finite; a program needn't handle non-finite values.
Results may differ from a plain program's by a relative error of at most 0.04.
Values may be sent and summed in bfloat16 or wider, within the bound.
No kernel may reach another device: no remote copies, remote signals or barrier semaphores. Data moves between devices by JAX's collectives and lax.ppermute only.
A program may use at most 128 MiB of HBM per device.

v0:
```python
import jax
import jax.numpy as jnp
from jax import lax
from jax.sharding import PartitionSpec as P

epsilon = 1e-05
highest = lax.Precision.HIGHEST


def silu_slope(argument):
    sigmoid_v = jax.nn.sigmoid(argument)
    return sigmoid_v * (1.0 + argument * (1.0 - sigmoid_v))


def normalize(features):
    average = jnp.mean(features, axis=-1, keepdims=True)
    centred = features - average
    inverse = lax.rsqrt(jnp.mean(centred * centred, axis=-1, keepdims=True) + epsilon)
    return (centred * inverse, inverse)


def normalize_back(features, upstream):
    normed, inverse = normalize(features)
    return inverse * (
        upstream
        - jnp.mean(upstream, axis=-1, keepdims=True)
        - normed * jnp.mean(upstream * normed, axis=-1, keepdims=True)
    )


def time_bias(lookup, stamps):
    highest_bucket = lookup.shape[-1] - 1
    distance = jnp.clip(stamps[:, None] - stamps[None, :], 0, highest_bucket)
    gathered_bias = jnp.zeros((lookup.shape[0],) + distance.shape, jnp.float32)
    for bucket in range(highest_bucket + 1):
        gathered_bias = jnp.where(
            (distance == bucket)[None], lookup[:, bucket][:, None, None], gathered_bias
        )
    return gathered_bias


def attend(activity, lookup, stamps, length):
    gate_part = activity[:, 0]
    value_part = activity[:, 1]
    query_part = activity[:, 2]
    key_part = activity[:, 3]
    scaling = query_part.shape[-1] ** (-0.5)
    scores = jnp.einsum(
        "ihk,jhk->hij", query_part, key_part, preferred_element_type=jnp.float32
    ) * scaling + time_bias(lookup, stamps)
    places = lax.iota(jnp.int32, activity.shape[0])
    allowed = ((places[None, :] <= places[:, None]) & (places[:, None] < length))[None]
    seq_count = length.astype(jnp.float32)
    weights = (jnp.where(allowed, jax.nn.silu(scores), 0.0) / seq_count).astype(jnp.bfloat16)
    attended = jnp.einsum("hij,jhk->ihk", weights, value_part, preferred_element_type=jnp.float32)
    normed, inverse = normalize(attended)
    return (
        gate_part,
        value_part,
        query_part,
        key_part,
        scaling,
        scores,
        allowed,
        seq_count,
        weights,
        normed,
        inverse,
    )


def mix_forward(activity, lookup, stamps, length):
    parts = attend(activity, lookup, stamps, length)
    return (parts[9] * parts[0].astype(jnp.float32)).astype(jnp.bfloat16)


def mix_backward(activity, lookup, stamps, length, upstream):
    (
        gate_part,
        value_part,
        query_part,
        key_part,
        scaling,
        scores,
        allowed,
        seq_count,
        weights,
        normed,
        inverse,
    ) = attend(activity, lookup, stamps, length)
    grad_gate = upstream * normed
    grad_normed = upstream * gate_part.astype(jnp.float32)
    grad_attended = inverse * (
        grad_normed
        - jnp.mean(grad_normed, axis=-1, keepdims=True)
        - normed * jnp.mean(grad_normed * normed, axis=-1, keepdims=True)
    )
    grad_attended = grad_attended.astype(jnp.bfloat16)
    grad_weights = jnp.einsum(
        "ihk,jhk->hij", grad_attended, value_part, preferred_element_type=jnp.float32
    )
    grad_value = jnp.einsum(
        "hij,ihk->jhk", weights, grad_attended, preferred_element_type=jnp.float32
    )
    grad_scores = (jnp.where(allowed, grad_weights * silu_slope(scores), 0.0) / seq_count).astype(
        jnp.bfloat16
    )
    grad_query = (
        jnp.einsum("hij,jhk->ihk", grad_scores, key_part, preferred_element_type=jnp.float32)
        * scaling
    )
    grad_key = (
        jnp.einsum("hij,ihk->jhk", grad_scores, query_part, preferred_element_type=jnp.float32)
        * scaling
    )
    return jnp.stack([grad_gate, grad_value, grad_query, grad_key], axis=1)


def share_rows(block):
    return lax.all_gather(block, "tp", axis=0, tiled=True)


def scatter_rows(term, own_rows):
    return lax.psum_scatter(
        term(jnp.int32(0), lax.axis_size("tp") * own_rows).astype(jnp.bfloat16),
        "tp",
        scatter_dimension=0,
        tiled=True,
    ).astype(jnp.float32)


def orthonormal(factors):
    gram = jnp.einsum("lhrn,lhsn->lhrs", factors, factors, precision=highest)
    lower = jnp.linalg.cholesky(gram)
    return lax.linalg.triangular_solve(lower, factors, left_side=True, lower=True)


def compress(grads_in, grads_out, errors_in, errors_out, start_in, start_out, replicas):
    merged_in = grads_in.astype(jnp.float32) + errors_in
    merged_out = grads_out.astype(jnp.float32) + errors_out
    left_in = jnp.einsum("lhrm,lhnm->lhrn", start_in, merged_in, precision=highest)
    left_out = jnp.einsum("lhrm,lhnm->lhrn", start_out, merged_out, precision=highest)
    left_in, left_out = (
        lax.psum(left_in.astype(jnp.bfloat16), "rep").astype(jnp.float32),
        lax.psum(left_out.astype(jnp.bfloat16), "rep").astype(jnp.float32),
    )
    basis_in = orthonormal(left_in)
    basis_out = orthonormal(left_out)
    right_in = jnp.einsum("lhrn,lhnm->lhrm", basis_in, merged_in, precision=highest)
    right_out = jnp.einsum("lhrn,lhnm->lhrm", basis_out, merged_out, precision=highest)
    right_in, right_out = (
        lax.psum(right_in.astype(jnp.bfloat16), "rep").astype(jnp.float32),
        lax.psum(right_out.astype(jnp.bfloat16), "rep").astype(jnp.float32),
    )
    right_in = right_in / replicas
    right_out = right_out / replicas
    update_in = jnp.einsum("lhrn,lhrm->lhnm", basis_in, right_in, precision=highest)
    update_out = jnp.einsum("lhrn,lhrm->lhnm", basis_out, right_out, precision=highest)
    return (
        update_in,
        update_out,
        right_in,
        right_out,
        merged_in - update_in,
        merged_out - update_out,
    )


def per_device(
    inputs,
    cotangent,
    weight_in,
    weight_out,
    bias_table,
    lengths,
    stamps,
    factor_in,
    factor_out,
    error_in,
    error_out,
):
    replicas = lax.axis_size("rep")
    sequences_here = lengths.shape[0]
    seq_length = stamps.shape[1]
    layer_count = weight_in.shape[0]
    model_width = weight_in.shape[1]
    local_heads = weight_in.shape[3]
    head_size = weight_in.shape[4]
    own_rows = inputs.shape[0]
    all_rows = sequences_here * seq_length
    stream = inputs.astype(jnp.float32)
    stored = []
    for layer_index in range(layer_count):
        normed = normalize(stream)[0].astype(jnp.bfloat16)
        normed_all = share_rows(normed)
        flat_in = weight_in[layer_index].reshape(model_width, -1)
        projected = jnp.dot(normed_all, flat_in, preferred_element_type=jnp.float32).reshape(
            all_rows, 4, local_heads, head_size
        )
        activity = jax.nn.silu(projected).astype(jnp.bfloat16)
        lookup = bias_table[layer_index]
        gated_rows = lax.map(
            lambda member: mix_forward(member[0], lookup, member[1], member[2]),
            (
                activity.reshape(sequences_here, seq_length, 4, local_heads, head_size),
                stamps,
                lengths,
            ),
        )
        gated_flat = gated_rows.reshape(all_rows, -1)
        flat_out = weight_out[layer_index].reshape(-1, model_width)

        def out_term(offset, amount):
            return jnp.dot(gated_flat, flat_out, preferred_element_type=jnp.float32)

        mixture = scatter_rows(out_term, own_rows)
        stored.append((stream, normed_all, projected, activity, gated_flat))
        stream = stream + mixture
    grad_stream = cotangent.astype(jnp.float32)
    pieces = []
    for layer_index in reversed(range(layer_count)):
        stream_here, normed_all, projected, activity, gated_flat = stored[layer_index]
        lookup = bias_table[layer_index]
        grad_half = grad_stream.astype(jnp.bfloat16)
        grad_all = share_rows(grad_half)
        flat_out = weight_out[layer_index].reshape(-1, model_width)
        grad_gated = lax.dot_general(
            grad_all, flat_out, (((1,), (1,)), ((), ())), preferred_element_type=jnp.float32
        )
        grad_weight_out = (
            jnp.einsum("rc,rd->cd", gated_flat, grad_all, preferred_element_type=jnp.float32)
            .astype(jnp.bfloat16)
            .reshape(local_heads, head_size, model_width)
        )
        grad_activity = lax.map(
            lambda member: mix_backward(member[0], lookup, member[1], member[2], member[3]),
            (
                activity.reshape(sequences_here, seq_length, 4, local_heads, head_size),
                stamps,
                lengths,
                grad_gated.reshape(sequences_here, seq_length, local_heads, head_size),
            ),
        )
        grad_projected = (
            grad_activity.reshape(all_rows, 4, local_heads, head_size) * silu_slope(projected)
        ).astype(jnp.bfloat16)
        grad_weight_in = (
            jnp.einsum(
                "rd,rchk->hdck", normed_all, grad_projected, preferred_element_type=jnp.float32
            )
            .astype(jnp.bfloat16)
            .reshape(local_heads, model_width, 4 * head_size)
        )
        if layer_index > 0:
            grad_flat = grad_projected.reshape(all_rows, -1)
            flat_in = weight_in[layer_index].reshape(model_width, -1)

            def back_term(offset, amount):
                return lax.dot_general(
                    grad_flat, flat_in, (((1,), (1,)), ((), ())), preferred_element_type=jnp.float32
                )

            grad_normed = scatter_rows(back_term, own_rows)
            grad_stream = grad_stream + normalize_back(stream_here, grad_normed)
        upper = layer_index + 1
        pieces.insert(
            0,
            compress(
                grad_weight_in[None],
                grad_weight_out[None],
                error_in[0, layer_index:upper],
                error_out[0, layer_index:upper],
                factor_in[layer_index:upper],
                factor_out[layer_index:upper],
                replicas,
            ),
        )
    results = tuple(
        (jnp.concatenate([piece[position] for piece in pieces], axis=0) for position in range(6))
    )
    update_in, update_out, next_in, next_out, error_in_next, error_out_next = results
    return (update_in, update_out, next_in, next_out, error_in_next[None], error_out_next[None])


def solution(mesh):
    placed = (
        P(("rep", "tp"), None),
        P(("rep", "tp"), None),
        P(None, None, None, "tp", None),
        P(None, "tp", None, None),
        P(None, "tp", None),
        P("rep"),
        P("rep", None),
        P(None, "tp", None, None),
        P(None, "tp", None, None),
        P("rep", None, "tp", None, None),
        P("rep", None, "tp", None, None),
    )
    return jax.shard_map(
        per_device,
        mesh=mesh,
        in_specs=placed,
        out_specs=(
            P(None, "tp", None, None),
            P(None, "tp", None, None),
            P(None, "tp", None, None),
            P(None, "tp", None, None),
            P("rep", None, "tp", None, None),
            P("rep", None, "tp", None, None),
        ),
        check_vma=False,
    )
```

profile of v0, /device:TPU:0, one launch (start us, length us, event | category | flops | bytes accessed | tf_op | source)
XLA Modules:
  0.0 561.9 jit_solution(13316236720362880578)
XLA Ops:
  13.5 3.2 fusion.203
  16.7 22.4 %all-gather.5.cloned.1.call-done = bf16[1024,1024]{1,0:T(8,128)(2,1)} async-done(((bf16[128,1024]{1,0:T(8,128)(2,1)}), bf16[1024,1024]{1,0:T(8,128)(2,1)}) %all-gather.5.cloned.1.call-update) | async-done | bytes 2097168 | tf_op jit(solution)/shard_map/all_gather | solution.py:120
  42.7 18.9 %divide_convert_fusion.3 = (bf16[1024,1024]{1,0:T(8,128)(2,1)S(1)}, f32[1024,1024]{1,0:T(8,128)}) fusion(f32[]{:T(128)S(6)} %convert_element_type.333, pred[1024]{0:T(1024)(128)(4,1)S(1)} %iota_compare_fusion.3, f32[]{:T(128)} %bitcast.24, f32[]{:T(128)} %bitcast.23, f32[]{:T(128)} %bitcast.22, f32[]{:T(128)} %bitcast.21, f32[]{:T(128)} %bitcast.20, ...), kind=kOutput, calls=%fused_computation.7 | convolution fusion | flops 315621376 | bytes 6825028 | tf_op jit(solution)/shard_map/while/body/eval_jaxpr/ihk,jhk->hij/dot_general | solution.py:48
  66.7 33.9 %reduce-scatter.3.cloned.1.call-done = bf16[128,1024]{1,0:T(8,128)(2,1)} async-done(((bf16[1024,1024]{1,0:T(8,128)(2,1)}), bf16[128,1024]{1,0:T(8,128)(2,1)}) %reduce-scatter.3.cloned.1.call-update) | async-done | bytes 262160 | tf_op jit(solution)/shard_map/reduce_scatter | solution.py:124
  106.3 22.7 %all-gather.9.cloned.1.call-done = bf16[1024,1024]{1,0:T(8,128)(2,1)} async-done(((bf16[128,1024]{1,0:T(8,128)(2,1)}), bf16[1024,1024]{1,0:T(8,128)(2,1)}) %all-gather.9.cloned.1.call-update) | async-done | bytes 2097168 | tf_op jit(solution)/shard_map/all_gather | solution.py:120
  128.9 3.1 fusion.91
  132.7 18.7 %divide_convert_fusion.2 = (bf16[1024,1024]{1,0:T(8,128)(2,1)S(1)}, f32[1024,1024]{1,0:T(8,128)}) fusion(f32[]{:T(128)S(6)} %convert_element_type.333, pred[1024]{0:T(1024)(128)(4,1)S(1)} %iota_compare_fusion.3, f32[]{:T(128)} %bitcast.52, f32[]{:T(128)} %bitcast.51, f32[]{:T(128)} %bitcast.50, f32[]{:T(128)} %bitcast.49, f32[]{:T(128)} %bitcast.48, ...), kind=kOutput, calls=%fused_computation.4 | convolution fusion | flops 315621376 | bytes 6825028 | tf_op jit(solution)/shard_map/while/body/eval_jaxpr/ihk,jhk->hij/dot_general | solution.py:48
  169.5 34.0 %reduce-scatter.5.cloned.1.call-done = bf16[128,1024]{1,0:T(8,128)(2,1)} async-done(((bf16[1024,1024]{1,0:T(8,128)(2,1)}), bf16[128,1024]{1,0:T(8,128)(2,1)}) %reduce-scatter.5.cloned.1.call-update) | async-done | bytes 262160 | tf_op jit(solution)/shard_map/reduce_scatter | solution.py:124
  207.2 5.2 fusion.45
  221.6 9.6 %all-gather.11.cloned.1.call-done = bf16[1024,1024]{1,0:T(8,128)(2,1)} async-done(((bf16[128,1024]{1,0:T(8,128)(2,1)}), bf16[1024,1024]{1,0:T(8,128)(2,1)}) %all-gather.11.cloned.1.call-update) | async-done | bytes 2097168 | tf_op jit(solution)/shard_map/all_gather | solution.py:120
  240.9 3.0 fusion.51
  243.8 3.1 copy.19
  246.9 4.9 fusion.69
  257.1 77.7 %all-reduce.11.cloned.1.call-done = (bf16[1,1,32,1024]{3,2,1,0:T(8,128)(2,1)}, bf16[1,1,32,1024]{3,2,1,0:T(8,128)(2,1)}) async-done(((bf16[1,1,32,1024]{3,2,1,0:T(8,128)(2,1)}, bf16[1,1,32,1024]{3,2,1,0:T(8,128)(2,1)}), (bf16[1,1,32,1024]{3,2,1,0:T(8,128)(2,1)}, bf16[1,1,32,1024]{3,2,1,0:T(8,128)(2,1)})) %all-reduce.11.cloned.1.call-update) | async-done | bytes 131088 | tf_op jit(solution)/shard_map/psum | solution.py:144
  337.0 2.9 custom-call.14
  343.8 2.9 custom-call.16
  351.8 3.6 fusion.80
  355.7 3.8 fusion.83
  361.4 3.0 copy.29
  364.4 76.4 %all-reduce.7.cloned.1.call-done = (bf16[1,1,32,512]{3,2,1,0:T(8,128)(2,1)}, bf16[1,1,32,512]{3,2,1,0:T(8,128)(2,1)}, bf16[1,1,32,128]{3,2,1,0:T(8,128)(2,1)}, bf16[1,1,32,128]{3,2,1,0:T(8,128)(2,1)}) async-done(((bf16[1,1,32,512]{3,2,1,0:T(8,128)(2,1)}, bf16[1,1,32,512]{3,2,1,0:T(8,128)(2,1)}, bf16[1,1,32,128]{3,2,1,0:T(8,128)(2,1)}, bf16[1,1,32,128]{3,2,1,0:T(8,128)(2,1)}), ...) | async-done | bytes 81936 | tf_op jit(solution)/shard_map/psum | solution.py:152
  445.0 3.9 fusion.159
  449.2 2.9 custom-call.18
  465.3 5.6 %fusion.22 = (f32[1,1,1024,512]{3,2,1,0:T(8,128)S(1)}, f32[1,1,1024,512]{3,2,1,0:T(8,128)S(1)}) fusion(f32[1024,512]{1,0:T(8,128)S(1)} %fusion.165, f32[1024,512]{1,0:T(8,128)} %copy.29, f32[1,2,1,1024,512]{4,3,2,1,0:T(8,128)} %param.25, f32[1024,512]{1,0:T(8,128)} %fusion.159, f32[1024,512]{1,0:T(8,128)} %copy.38), kind=kLoop, calls=%fused_computation.39 | loop fusion | flops 2097152 | bytes 16777216 | tf_op jit(solution)/shard_map/sub | solution.py:164
  476.5 70.8 %all-reduce.9.cloned.1.call-done = (bf16[1,1,32,1024]{3,2,1,0:T(8,128)(2,1)}, bf16[1,1,32,1024]{3,2,1,0:T(8,128)(2,1)}) async-done(((bf16[1,1,32,1024]{3,2,1,0:T(8,128)(2,1)}, bf16[1,1,32,1024]{3,2,1,0:T(8,128)(2,1)}), (bf16[1,1,32,1024]{3,2,1,0:T(8,128)(2,1)}, bf16[1,1,32,1024]{3,2,1,0:T(8,128)(2,1)})) %all-reduce.9.cloned.1.call-update) | async-done | bytes 131088 | tf_op jit(solution)/shard_map/psum | solution.py:153
  (205 shorter events, 110.0 us)
Async XLA Ops:
  7.2 32.0 %all-gather.5.cloned.1.call-start = ((), (), s32[]{:S(2)}) async-start(), calls=%async_computation.2 | async-start | bytes 2359296 | tf_op jit(solution)/shard_map/all_gather | solution.py:120
  11.4 89.3 %reduce-scatter.3.cloned.1.call-start = ((), (), s32[]{:S(2)}) async-start(), calls=%async_computation.3 | async-start | bytes 2359296 | tf_op jit(solution)/shard_map/reduce_scatter | solution.py:124
  12.1 148.6 %copy-start.35 = (pred[1024]{0:T(1024)(128)(4,1)}, pred[1024]{0:T(1024)(128)(4,1)S(1)}, u32[]{:S(2)}) copy-start(pred[1024]{0:T(1024)(128)(4,1)S(1)} %iota_compare_fusion.3) | copy-start | bytes 3076
  42.1 19.5 %copy-start.19 = (f32[1024,512]{0,1:T(8,128)}, f32[1024,512]{0,1:T(8,128)S(1)}, u32[]{:S(2)}) copy-start(f32[1024,512]{0,1:T(8,128)S(1)} %fusion.93) | copy-start | bytes 6291460
  42.6 21.2 %copy-start.13 = (bf16[1024,4,1,128]{0,3,2,1:T(8,128)(2,1)}, bf16[1024,4,1,128]{0,3,2,1:T(8,128)(2,1)S(1)}, u32[]{:S(2)}) copy-start(bf16[1024,4,1,128]{0,3,2,1:T(8,128)(2,1)S(1)} %multiply_convert_fusion.1) | copy-start | bytes 3145732
  62.8 37.8 %copy-start.3 = (bf16[128,1024]{1,0:T(8,128)(2,1)S(1)}, bf16[128,1024]{1,0:T(8,128)(2,1)}, u32[]{:S(2)}) copy-start(bf16[128,1024]{1,0:T(8,128)(2,1)} %param.16) | copy-start | bytes 786436
  66.7 62.3 %all-gather.9.cloned.1.call-start = ((), (), s32[]{:S(2)}) async-start(), calls=%async_computation.5 | async-start | bytes 2359296 | tf_op jit(solution)/shard_map/all_gather | solution.py:120
  104.8 51.2 %all-gather.7.cloned.1.call-start = ((), (), s32[]{:S(2)}) async-start(), calls=%async_computation.4 | async-start | bytes 2359296 | tf_op jit(solution)/shard_map/all_gather | solution.py:120
  105.3 98.1 %reduce-scatter.5.cloned.1.call-start = ((), (), s32[]{:S(2)}) async-start(), calls=%async_computation.6 | async-start | bytes 2359296 | tf_op jit(solution)/shard_map/reduce_scatter | solution.py:124
  132.6 18.7 %copy-start.15 = (bf16[1024,4,1,128]{0,3,2,1:T(8,128)(2,1)}, bf16[1024,4,1,128]{0,3,2,1:T(8,128)(2,1)S(1)}, u32[]{:S(2)}) copy-start(bf16[1024,4,1,128]{0,3,2,1:T(8,128)(2,1)S(1)} %multiply_convert_fusion) | copy-start | bytes 3145732
  169.5 61.7 %all-gather.11.cloned.1.call-start = ((), (), s32[]{:S(2)}) async-start(), calls=%async_computation.7 | async-start | bytes 2359296 | tf_op jit(solution)/shard_map/all_gather | solution.py:120
  206.9 127.8 %all-reduce.11.cloned.1.call-start = ((), (), s32[]{:S(2)}) async-start(), calls=%async_computation.10 | async-start | bytes 262144 | tf_op jit(solution)/shard_map/psum | solution.py:144
  212.4 5.2 copy-start.29
  212.4 6.4 %copy-start.30 = (f32[2,1,32,512]{3,2,1,0:T(8,128)S(1)}, f32[2,1,32,512]{3,2,1,0:T(8,128)}, u32[]{:S(2)}) copy-start(f32[2,1,32,512]{3,2,1,0:T(8,128)} %param.23) | copy-start | bytes 393220
  221.6 14.2 %copy-start.36 = (pred[1024]{0:T(1024)(128)(4,1)S(1)}, pred[1024]{0:T(1024)(128)(4,1)}, u32[]{:S(2)}) copy-start(pred[1024]{0:T(1024)(128)(4,1)} %copy-done.35) | copy-start | bytes 3076
  243.8 8.3 %copy-start.18 = (bf16[1024,128]{0,1:T(8,128)(2,1)S(1)}, bf16[1024,128]{0,1:T(8,128)(2,1)}, u32[]{:S(2)}) copy-start(bf16[1024,128]{0,1:T(8,128)(2,1)} %copy-done.17) | copy-start | bytes 786436
  243.8 8.3 %copy-start.26 = (f32[1,2,1,128,1024]{4,3,2,1,0:T(8,128)S(1)}, f32[1,2,1,128,1024]{4,3,2,1,0:T(8,128)}, u32[]{:S(2)}) copy-start(f32[1,2,1,128,1024]{4,3,2,1,0:T(8,128)} %param.26) | copy-start | bytes 3145732
  251.8 189.0 %all-reduce.7.cloned.1.call-start = ((), (), s32[]{:S(2)}) async-start(), calls=%async_computation.8 | async-start | bytes 163840 | tf_op jit(solution)/shard_map/psum | solution.py:152
  350.5 5.2 copy-start.1
  359.5 187.8 %all-reduce.9.cloned.1.call-start = ((), (), s32[]{:S(2)}) async-start(), calls=%async_computation.9 | async-start | bytes 262144 | tf_op jit(solution)/shard_map/psum | solution.py:153
  361.4 101.8 %copy-start.5 = (f32[128,1024]{1,0:T(8,128)S(1)}, f32[128,1024]{1,0:T(8,128)}, u32[]{:S(2)}) copy-start(f32[128,1024]{1,0:T(8,128)} %copy-done.4) | copy-start | bytes 1572868
  361.4 102.8 %copy-start.12 = (f32[128,1024]{1,0:T(8,128)S(1)}, f32[128,1024]{1,0:T(8,128)}, u32[]{:S(2)}) copy-start(f32[128,1024]{1,0:T(8,128)} %copy-done.11) | copy-start | bytes 1572868
  440.8 8.1 %copy-start.31 = (bf16[1,1,32,128]{3,2,1,0:T(8,128)(2,1)S(1)}, bf16[1,1,32,128]{3,2,1,0:T(8,128)(2,1)}, u32[]{:S(2)}) copy-start(bf16[1,1,32,128]{3,2,1,0:T(8,128)(2,1)} %get-tuple-element.90) | copy-start | bytes 24580
  440.8 8.2 %copy-start.32 = (bf16[1,1,32,128]{3,2,1,0:T(8,128)(2,1)S(1)}, bf16[1,1,32,128]{3,2,1,0:T(8,128)(2,1)}, u32[]{:S(2)}) copy-start(bf16[1,1,32,128]{3,2,1,0:T(8,128)(2,1)} %get-tuple-element.91) | copy-start | bytes 24580
  (24 other events, 68.7 us)
Sparse Core Ops, SparseCore 0:
  11.5 27.6 all-gather.4
  66.8 33.8 reduce-scatter.2
  104.9 24.0 all-gather.8
  130.5 25.4 all-gather.6
  169.6 33.8 reduce-scatter.4
  207.0 24.0 all-gather.10
  251.9 82.7 all-reduce.10
  359.6 81.1 all-reduce.6
  465.4 81.8 all-reduce.8
where the time goes:
time: 569 us; the launch traced here: 562 us
  waiting for transfers between devices  351 us (62%)
  matrix products  111 us (20%)
  other arithmetic  61.1 us (11%)
  local copies, waits for them, and re-layouts  22.5 us (4%)
  between operations  15.7 us (3%)
    psum x1, waiting for transfers between devices, compress(): lax.psum(left_in.astype(jnp.bfloat16), 'rep').astype(jnp.float32)  77.7 us
    psum x1, waiting for transfers between devices, compress(): lax.psum(right_in.astype(jnp.bfloat16), 'rep').astype(jnp.float32)  76.4 us
    psum x1, waiting for transfers between devices, compress(): lax.psum(right_out.astype(jnp.bfloat16), 'rep').astype(jnp.float32)  70.8 us
    reduce_scatter x2, waiting for transfers between devices, scatter_rows(): lax.psum_scatter(term(jnp.int32(0), lax.axis_size('tp') * own_rows).astyp...  67.9 us
    all_gather x4, waiting for transfers between devices, share_rows(): return lax.all_gather(block, 'tp', axis=0, tiled=True)  57.1 us
    dot_general x2, matrix products, attend(): jnp.einsum('ihk,jhk->hij', query_part, key_part, preferred_element_type=j...  37.5 us
    another operation x12, other arithmetic, orthonormal(): lower = jnp.linalg.cholesky(gram)  14.4 us
    another operation x8, other arithmetic, orthonormal(): lax.linalg.triangular_solve(lower, factors, left_side=True, lower=True)  12.3 us
  transfers between devices with their start and end apart: 9, of which 9 were waited for; matrix products, arithmetic and copies ran while one was open for 11% of the time, Pallas kernels for 0%

commit v1 on v0

v1 whole, which is shorter than its diff:
```python
import functools

import jax
import jax.numpy as jnp
from jax import lax
from jax.experimental import pallas as pl
from jax.experimental.pallas import tpu as pltpu
from jax.sharding import PartitionSpec as P

epsilon = 1e-05
highest = lax.Precision.HIGHEST
half = jnp.bfloat16
full = jnp.float32

TOKENS = 1024
WIDTH = 1024
HEAD = 128
WIDE = 4 * HEAD
RANK = 32
BUCKETS = 16
OWN = 128
BLOCK = 256
BLOCKS = TOKENS // BLOCK
VMEM_BYTES = 56 * 1024 * 1024

whole = pl.BlockSpec(memory_space=pltpu.VMEM)
scalars = pl.BlockSpec(memory_space=pltpu.SMEM)


def nn(a, b):
    return jnp.dot(a, b, preferred_element_type=full)


def nt(a, b, precision=None):
    return lax.dot_general(
        a, b, (((1,), (1,)), ((), ())), preferred_element_type=full, precision=precision
    )


def tn(a, b, precision=None):
    return lax.dot_general(
        a, b, (((0,), (0,)), ((), ())), preferred_element_type=full, precision=precision
    )


def logistic(x):
    return 0.5 * jnp.tanh(0.5 * x) + 0.5


def silu_slope(x):
    s = logistic(x)
    return s * (1.0 + x * (1.0 - s))


def centre(x):
    c = x - jnp.mean(x, axis=-1, keepdims=True)
    inverse = lax.rsqrt(jnp.mean(c * c, axis=-1, keepdims=True) + epsilon)
    return c * inverse, inverse


def split(x):
    high = x.astype(half)
    return high, (x - high.astype(full)).astype(half)


def call(body, name, flops, moved, operands, in_specs, outs, scratch, out_specs=None):
    grid = {} if all(spec.block_shape is None for spec in in_specs) else {"grid": (1,)}
    return pl.pallas_call(
        body,
        name=name,
        **grid,
        out_shape=outs,
        in_specs=in_specs,
        out_specs=out_specs if out_specs is not None else [whole] * len(outs),
        scratch_shapes=scratch,
        compiler_params=pltpu.CompilerParams(vmem_limit_bytes=VMEM_BYTES),
        cost_estimate=pl.CostEstimate(flops=flops, bytes_accessed=moved, transcendentals=0),
    )(*operands)


def shape(dims, dtype):
    return jax.ShapeDtypeStruct(dims, dtype)


def placed(device, position):
    base = device if position < 4 else device + 1 - 2 * lax.rem(device, 2)
    return lax.rem(base + 2 * (position % 4), 8)


def rows_of(device, position):
    return pl.ds(pl.multiple_of(placed(device, position) * OWN, OWN), OWN)


def attention_operands(stamps_ref, table_ref, query_of, key_of, qa_ref, ka_ref):
    scale = HEAD**-0.5
    places = lax.broadcasted_iota(jnp.int32, (HEAD, HEAD), 0)
    lanes = lax.broadcasted_iota(jnp.int32, (HEAD, HEAD), 1)
    gap = jnp.clip(places - (lanes & 63), 0, BUCKETS - 1)
    lookup = jnp.zeros((HEAD, HEAD), full)
    for bucket in range(BUCKETS):
        lookup = jnp.where(gap == bucket, table_ref[0, bucket] * (1.0 / scale), lookup)
    high = lookup.astype(half).astype(full)
    lookup = jnp.where(lanes < 64, high, lookup - high)
    lookup = jnp.where(places < 64, lookup, 0.0).astype(half)
    first = stamps_ref[0:1, :]
    for part in range(BLOCKS):
        rows = slice(part * BLOCK, (part + 1) * BLOCK)
        since = stamps_ref[rows, :] - first
        columns = lax.broadcasted_iota(jnp.int32, (BLOCK, HEAD), 1)
        hot = jnp.where(since == (columns & 63), 1.0, 0.0)
        left_hot = jnp.where(columns < 64, hot, 0.0).astype(half)
        qa_ref[rows, HEAD:] = nn(left_hot, lookup).astype(half)
        ka_ref[rows, HEAD:] = hot.astype(half)
        qa_ref[rows, :HEAD] = query_of(rows)
        ka_ref[rows, :HEAD] = key_of(rows)


def score_block(qa_ref, ka_ref, i, j):
    return nt(
        qa_ref[i * BLOCK : (i + 1) * BLOCK, :], ka_ref[j * BLOCK : (j + 1) * BLOCK, :]
    ) * (HEAD**-0.5)


def causal():
    return lax.broadcasted_iota(jnp.int32, (BLOCK, BLOCK), 0) >= lax.broadcasted_iota(
        jnp.int32, (BLOCK, BLOCK), 1
    )


def row_mask(i, length):
    places = lax.broadcasted_iota(jnp.int32, (BLOCK, HEAD), 0) + i * BLOCK
    return places < length


def attend_forward(length, qa_ref, ka_ref, values_ref, proj_ref, gated_ref):
    share = 1.0 / length.astype(full)
    for i in range(BLOCKS):
        rows = slice(i * BLOCK, (i + 1) * BLOCK)
        total = jnp.zeros((BLOCK, HEAD), full)
        for j in range(i + 1):
            s = score_block(qa_ref, ka_ref, i, j)
            w = s * logistic(s)
            if i == j:
                w = jnp.where(causal(), w, 0.0)
            total += nn(w.astype(half), values_ref[j * BLOCK : (j + 1) * BLOCK, :])
        attended = jnp.where(row_mask(i, length), total * share, 0.0)
        normed, _ = centre(attended)
        gate = proj_ref[rows, :HEAD]
        gate = (gate * logistic(gate)).astype(half).astype(full)
        gated_ref[rows, :] = (normed * gate).astype(half)


def attend_backward(
    length,
    qa_ref,
    ka_ref,
    values_ref,
    proj_ref,
    upstream_of,
    gated_ref,
    grad_ref,
    weights_ref,
    slope_ref,
    dk_ref,
    dv_ref,
):
    share = 1.0 / length.astype(full)
    scale = HEAD**-0.5
    for i in range(BLOCKS):
        rows = slice(i * BLOCK, (i + 1) * BLOCK)
        total = jnp.zeros((BLOCK, HEAD), full)
        for j in range(i + 1):
            cols = slice(j * BLOCK, (j + 1) * BLOCK)
            s = score_block(qa_ref, ka_ref, i, j)
            sigmoid = logistic(s)
            w = s * sigmoid
            slope = sigmoid + w * (1.0 - sigmoid)
            if i == j:
                w = jnp.where(causal(), w, 0.0)
                slope = jnp.where(causal(), slope, 0.0)
            w = w.astype(half)
            weights_ref[:, cols] = w
            slope_ref[:, cols] = slope
            total += nn(w, values_ref[cols, :])
        inside = row_mask(i, length)
        attended = jnp.where(inside, total * share, 0.0)
        normed, inverse = centre(attended)
        gate_raw = proj_ref[rows, :HEAD]
        gate = (gate_raw * logistic(gate_raw)).astype(half).astype(full)
        gated_ref[rows, :] = (normed * gate).astype(half)
        upstream = upstream_of(rows)
        grad_ref[rows, :HEAD] = (upstream * normed * silu_slope(gate_raw)).astype(half)
        g = upstream * gate
        back = inverse * (
            g
            - jnp.mean(g, axis=-1, keepdims=True)
            - normed * jnp.mean(g * normed, axis=-1, keepdims=True)
        )
        back = jnp.where(inside, back, 0.0).astype(half)
        dq = jnp.zeros((BLOCK, HEAD), full)
        for j in range(i + 1):
            cols = slice(j * BLOCK, (j + 1) * BLOCK)
            ds = (nt(back, values_ref[cols, :]) * slope_ref[:, cols]).astype(half)
            dq += nn(ds, ka_ref[cols, :HEAD])
            dk = tn(ds, qa_ref[rows, :HEAD])
            dv = tn(weights_ref[:, cols], back)
            if i == j:
                dk_ref[cols, :] = dk
                dv_ref[cols, :] = dv
            else:
                dk_ref[cols, :] += dk
                dv_ref[cols, :] += dv
        raw = proj_ref[rows, 2 * HEAD : 3 * HEAD]
        grad_ref[rows, 2 * HEAD : 3 * HEAD] = (dq * (scale * share) * silu_slope(raw)).astype(half)
    for i in range(BLOCKS):
        rows = slice(i * BLOCK, (i + 1) * BLOCK)
        raw = proj_ref[rows, HEAD : 2 * HEAD]
        grad_ref[rows, HEAD : 2 * HEAD] = (dv_ref[rows, :] * share * silu_slope(raw)).astype(half)
        raw = proj_ref[rows, 3 * HEAD :]
        grad_ref[rows, 3 * HEAD :] = (dk_ref[rows, :] * (scale * share) * silu_slope(raw)).astype(
            half
        )


def silu_half(x):
    return (x * logistic(x)).astype(half)


def operands_from(proj_ref, stamps_ref, table_ref, qa_ref, ka_ref, values_ref):
    attention_operands(
        stamps_ref,
        table_ref,
        lambda rows: silu_half(proj_ref[rows, 2 * HEAD : 3 * HEAD]),
        lambda rows: silu_half(proj_ref[rows, 3 * HEAD :]),
        qa_ref,
        ka_ref,
    )
    for part in range(BLOCKS):
        rows = slice(part * BLOCK, (part + 1) * BLOCK)
        values_ref[rows, :] = silu_half(proj_ref[rows, HEAD : 2 * HEAD])


def first_forward(device_ref, length_ref, table_ref, stamps_ref, *refs):
    blocks = refs[:8]
    weight_ref, rows_ref, normed_ref, proj_ref, gated_ref, qa_ref, ka_ref, values_ref = refs[8:]
    device = device_ref[0]
    for position, block in enumerate(blocks):
        rows_ref[rows_of(device, position), :] = block[...]
    for part in range(BLOCKS):
        rows = slice(part * BLOCK, (part + 1) * BLOCK)
        normed = centre(rows_ref[rows, :].astype(full))[0].astype(half)
        normed_ref[rows, :] = normed
        proj_ref[rows, :] = nn(normed, weight_ref[...])
    operands_from(proj_ref, stamps_ref, table_ref, qa_ref, ka_ref, values_ref)
    attend_forward(length_ref[0], qa_ref, ka_ref, values_ref, proj_ref, gated_ref)


def second_layer(device_ref, length_ref, table_ref, stamps_ref, rows_ref, *refs):
    heads = refs[:8]
    mix_ref, weight_in_ref, cot_ref, weight_out_ref = refs[8:12]
    normed_ref, grad_ref, gated_ref, send_ref, keep_ref, stream_ref = refs[12:18]
    all_ref, proj_ref, qa_ref, ka_ref, values_ref = refs[18:23]
    weights_ref, slope_ref, dk_ref, dv_ref, whole_stream_ref = refs[23:]
    device = device_ref[0]
    for position, block in enumerate(heads):
        all_ref[:, rows_of(device, position)] = block[...]
    for part in range(BLOCKS):
        rows = slice(part * BLOCK, (part + 1) * BLOCK)
        stream = rows_ref[rows, :].astype(full) + nn(all_ref[rows, :], mix_ref[...])
        whole_stream_ref[rows, :] = stream
        normed = centre(stream)[0].astype(half)
        normed_ref[rows, :] = normed
        proj_ref[rows, :] = nn(normed, weight_in_ref[...])
    stream_ref[...] = whole_stream_ref[rows_of(device, 0), :]
    operands_from(proj_ref, stamps_ref, table_ref, qa_ref, ka_ref, values_ref)
    attend_backward(
        length_ref[0],
        qa_ref,
        ka_ref,
        values_ref,
        proj_ref,
        lambda rows: nt(cot_ref[rows, :], weight_out_ref[...]),
        gated_ref,
        grad_ref,
        weights_ref,
        slope_ref,
        dk_ref,
        dv_ref,
    )
    for position in range(4):
        out = slice(position * OWN, (position + 1) * OWN)
        keep_ref[out, :] = nt(grad_ref[rows_of(device, position), :], weight_in_ref[...]).astype(half)
        send_ref[out, :] = nt(
            grad_ref[rows_of(device, position + 4), :], weight_in_ref[...]
        ).astype(half)


def pair_sum(keep_ref, come_ref, a_ref, b_ref, c_ref, d_ref):
    for position, out in enumerate((a_ref, b_ref, c_ref, d_ref)):
        rows = slice(position * OWN, (position + 1) * OWN)
        out[...] = (keep_ref[rows, :].astype(full) + come_ref[rows, :].astype(full)).astype(half)


def norm_backward(a_ref, b_ref, c_ref, d_ref, stream_ref, cot_ref, grad_ref):
    upstream = (a_ref[...].astype(full) + c_ref[...].astype(full)) + (
        b_ref[...].astype(full) + d_ref[...].astype(full)
    )
    normed, inverse = centre(stream_ref[...])
    grad = cot_ref[...].astype(full) + inverse * (
        upstream
        - jnp.mean(upstream, axis=-1, keepdims=True)
        - normed * jnp.mean(upstream * normed, axis=-1, keepdims=True)
    )
    grad_ref[...] = grad.astype(half)


def merge(
    normed_ref,
    grad_ref,
    gated_ref,
    top_ref,
    error_in_ref,
    error_out_ref,
    factor_in_ref,
    factor_out_ref,
    merged_in_ref,
    merged_out_ref,
    left_ref,
    left_rows,
):
    merged_in = tn(normed_ref[...], grad_ref[...]).astype(half).astype(full) + error_in_ref[0]
    merged_in_ref[...] = merged_in
    left_ref[left_rows, :WIDTH] = left_product(factor_in_ref[0], merged_in).astype(half)
    merged_out = tn(gated_ref[...], top_ref[...]).astype(half).astype(full) + error_out_ref[0]
    merged_out_ref[...] = merged_out
    left_ref[left_rows, WIDTH:] = left_product(factor_out_ref[0], merged_out).astype(half)


def left_product(factor, merged):
    high, low = split(merged)
    factor_high, factor_low = split(factor)
    both = nt(jnp.concatenate([factor_high, factor_low], axis=0), high)
    return both[:RANK] + both[RANK:] + nt(factor_high, low)


def second_merge(
    normed_ref,
    grad_ref,
    gated_ref,
    cot_ref,
    error_in_ref,
    error_out_ref,
    factor_in_ref,
    factor_out_ref,
    merged_in_ref,
    merged_out_ref,
    left_ref,
):
    merge(
        normed_ref,
        grad_ref,
        gated_ref,
        cot_ref,
        error_in_ref,
        error_out_ref,
        factor_in_ref,
        factor_out_ref,
        merged_in_ref,
        merged_out_ref,
        left_ref,
        slice(0, RANK),
    )


def first_backward(device_ref, length_ref, table_ref, stamps_ref, proj_ref, normed_ref, *refs):
    blocks = refs[:8]
    weight_out_ref, error_in_ref, error_out_ref, factor_in_ref, factor_out_ref, other_ref = refs[8:14]
    merged_in_ref, merged_out_ref, left_ref = refs[14:17]
    top_ref, grad_ref, gated_ref, qa_ref, ka_ref, values_ref = refs[17:23]
    weights_ref, slope_ref, dk_ref, dv_ref = refs[23:]
    device = device_ref[0]
    for position, block in enumerate(blocks):
        top_ref[rows_of(device, position), :] = block[...]
    operands_from(proj_ref, stamps_ref, table_ref, qa_ref, ka_ref, values_ref)
    attend_backward(
        length_ref[0],
        qa_ref,
        ka_ref,
        values_ref,
        proj_ref,
        lambda rows: nt(top_ref[rows, :], weight_out_ref[...]),
        gated_ref,
        grad_ref,
        weights_ref,
        slope_ref,
        dk_ref,
        dv_ref,
    )
    left_ref[RANK:, :] = other_ref[...]
    merge(
        normed_ref,
        grad_ref,
        gated_ref,
        top_ref,
        error_in_ref,
        error_out_ref,
        factor_in_ref,
        factor_out_ref,
        merged_in_ref,
        merged_out_ref,
        left_ref,
        slice(0, RANK),
    )


def four_sum(a_ref, b_ref, c_ref, d_ref, rows, columns):
    return (a_ref[rows, columns].astype(full) + c_ref[rows, columns].astype(full)) + (
        b_ref[rows, columns].astype(full) + d_ref[rows, columns].astype(full)
    )


def ring_sum(a_ref, b_ref, c_ref, d_ref, out_ref):
    everything = slice(None)
    out_ref[...] = four_sum(a_ref, b_ref, c_ref, d_ref, everything, everything).astype(half)


def cholesky_inverses(grams):
    shape_ = (RANK, 2 * RANK)
    places = lax.broadcasted_iota(jnp.int32, shape_, 0)
    unit = jnp.where(
        lax.broadcasted_iota(jnp.int32, (RANK, RANK), 0)
        == lax.broadcasted_iota(jnp.int32, (RANK, RANK), 1),
        1.0,
        0.0,
    )
    work = [jnp.concatenate([gram, unit], axis=1) for gram in grams]
    for k in range(RANK):
        for m in range(len(work)):
            a = work[m]
            root = lax.rsqrt(a[k : k + 1, k : k + 1])
            row = a[k : k + 1, :] * root
            column = jnp.where(places > k, a[:, k : k + 1] * root, 0.0)
            work[m] = jnp.where(places == k, row, a - column * row)
    return [a[:, RANK:] for a in work]


def basis_right(*refs):
    sums = refs[:4]
    merged_refs = refs[4:8]
    basis_ref, right_ref = refs[8:]
    lefts = []
    for layer in range(2):
        rows = slice(layer * RANK, (layer + 1) * RANK)
        lefts.append(four_sum(*sums, rows, slice(0, WIDTH)))
        lefts.append(four_sum(*sums, rows, slice(WIDTH, WIDTH + HEAD)))
    inverses = cholesky_inverses([nt(left, left, highest) for left in lefts])
    for position in range(4):
        layer, out = divmod(position, 2)
        rows = slice(layer * RANK, (layer + 1) * RANK)
        columns = slice(WIDTH, WIDTH + HEAD) if out else slice(0, WIDTH)
        basis = jnp.dot(
            inverses[position], lefts[position], preferred_element_type=full, precision=highest
        )
        basis_ref[rows, columns] = basis
        high, low = split(merged_refs[position][...])
        basis_high, basis_low = split(basis)
        both = nn(jnp.concatenate([basis_high, basis_low], axis=0), high)
        right = both[:RANK] + both[RANK:] + nn(basis_high, low)
        columns = slice(WIDE, WIDE + WIDTH) if out else slice(0, WIDE)
        right_ref[rows, columns] = right.astype(half)


def finish(*refs):
    sums = refs[:4]
    basis_ref = refs[4]
    merged_refs = refs[5:9]
    update_in, update_out, next_in, next_out, error_in, error_out = refs[9:]
    for position in range(4):
        layer, out = divmod(position, 2)
        rows = slice(layer * RANK, (layer + 1) * RANK)
        columns = slice(WIDTH, WIDTH + HEAD) if out else slice(0, WIDTH)
        update_ref, next_ref, error_ref = (
            (update_out, next_out, error_out) if out else (update_in, next_in, error_in)
        )
        basis_high, basis_low = split(basis_ref[rows, columns])
        columns = slice(WIDE, WIDE + WIDTH) if out else slice(0, WIDE)
        right = four_sum(*sums, rows, columns) * (1.0 / 16)
        next_ref[layer] = right
        right_high, right_low = split(right)
        update = tn(
            jnp.concatenate([basis_high, basis_high, basis_low], axis=0),
            jnp.concatenate([right_high, right_low, right_high], axis=0),
        )
        update_ref[layer] = update
        error_ref[layer] = merged_refs[position][...] - update


def send_tp(x, chips):
    return lax.ppermute(x, "tp", [(k, (k - 2 * chips) % 8) for k in range(8)])


def swap(x):
    return lax.ppermute(x, "tp", [(k, k ^ 1) for k in range(8)])


def gather_tp(x):
    mine = [x] + [send_tp(x, chips) for chips in (1, 2, 3)]
    return mine + [swap(block) for block in mine]


def ring_z(x):
    return [x] + [
        lax.ppermute(x, "rep", [(k, k - k % 4 + (k - step) % 4) for k in range(16)])
        for step in (1, 2, 3)
    ]


def ring_x(x):
    return [x] + [
        lax.ppermute(x, "rep", [(k, (k - 4 * step) % 16) for k in range(16)]) for step in (1, 2, 3)
    ]


def sum_rep(x):
    parts = ring_z(x)
    part = call(
        ring_sum,
        "ring_sum",
        x.size * 4,
        x.size * 10,
        parts,
        [whole] * 4,
        [shape(x.shape, half)],
        [],
    )[0]
    return ring_x(part)


def layer_block(dims, layer):
    return pl.BlockSpec((1,) + dims, lambda step: (layer, 0, 0))


def per_device(
    inputs,
    cotangent,
    weight_in,
    weight_out,
    bias_table,
    lengths,
    stamps,
    factor_in,
    factor_out,
    error_in,
    error_out,
):
    device = lax.axis_index("tp").astype(jnp.int32).reshape(1)
    stamps = stamps.reshape(TOKENS, 1)
    weight_in = weight_in.reshape(2, WIDTH, WIDE)
    weight_out = weight_out.reshape(2, HEAD, WIDTH)
    factor_in = factor_in.reshape(2, RANK, WIDE)
    factor_out = factor_out.reshape(2, RANK, WIDTH)
    error_in = error_in.reshape(2, WIDTH, WIDE)
    error_out = error_out.reshape(2, HEAD, WIDTH)

    input_blocks = gather_tp(inputs)
    mix_all = lax.all_gather(weight_out[0], "tp", axis=0, tiled=True)
    cot_all = lax.all_gather(cotangent, "tp", axis=0, tiled=True)

    attention_scratch = [
        pltpu.VMEM((TOKENS, 2 * HEAD), half),
        pltpu.VMEM((TOKENS, 2 * HEAD), half),
        pltpu.VMEM((TOKENS, HEAD), half),
    ]
    backward_scratch = [
        pltpu.VMEM((BLOCK, TOKENS), half),
        pltpu.VMEM((BLOCK, TOKENS), full),
        pltpu.VMEM((TOKENS, HEAD), full),
        pltpu.VMEM((TOKENS, HEAD), full),
    ]
    dot_flops = 2 * TOKENS * WIDTH * WIDE

    rows_all, normed_0, proj_0, gated_0 = call(
        first_forward,
        "first_forward",
        3 * dot_flops,
        12 << 20,
        (device, lengths, bias_table[0], stamps, *input_blocks, weight_in[0]),
        [scalars] * 3 + [whole] * 10,
        [
            shape((TOKENS, WIDTH), half),
            shape((TOKENS, WIDTH), half),
            shape((TOKENS, WIDE), full),
            shape((TOKENS, HEAD), half),
        ],
        attention_scratch,
    )
    gated_blocks = gather_tp(gated_0)

    normed_1, grad_1, gated_1, send, keep, stream = call(
        second_layer,
        "second_layer",
        10 * dot_flops,
        18 << 20,
        (
            device,
            lengths,
            bias_table[1],
            stamps,
            rows_all,
            *gated_blocks,
            mix_all,
            weight_in[1],
            cot_all,
            weight_out[1],
        ),
        [scalars] * 3 + [whole] * 14,
        [
            shape((TOKENS, WIDTH), half),
            shape((TOKENS, WIDE), half),
            shape((TOKENS, HEAD), half),
            shape((TOKENS // 2, WIDTH), half),
            shape((TOKENS // 2, WIDTH), half),
            shape((OWN, WIDTH), full),
        ],
        [
            pltpu.VMEM((TOKENS, WIDTH), half),
            pltpu.VMEM((TOKENS, WIDE), full),
            *attention_scratch,
            *backward_scratch,
            pltpu.VMEM((TOKENS, WIDTH), full),
        ],
    )
    come = swap(send)
    sums = call(
        pair_sum,
        "pair_sum",
        TOKENS * WIDTH,
        3 << 20,
        (keep, come),
        [whole] * 2,
        [shape((OWN, WIDTH), half)] * 4,
        [],
    )
    parts = [sums[0]] + [
        lax.ppermute(sums[chips], "tp", [(k, (k + 2 * chips) % 8) for k in range(8)])
        for chips in (1, 2, 3)
    ]
    grad_own = call(
        norm_backward,
        "norm_backward",
        OWN * WIDTH * 20,
        2 << 20,
        (*parts, stream, cotangent),
        [whole] * 6,
        [shape((OWN, WIDTH), half)],
        [],
    )[0]
    grad_blocks = gather_tp(grad_own)

    merge_specs = [
        (layer_block((WIDTH, WIDE), layer), layer_block((HEAD, WIDTH), layer))
        + (layer_block((RANK, WIDE), layer), layer_block((RANK, WIDTH), layer))
        for layer in range(2)
    ]
    merged_shapes = [shape((WIDTH, WIDE), full), shape((HEAD, WIDTH), full)]
    merged_in_1, merged_out_1, left_1 = call(
        second_merge,
        "second_merge",
        3 * dot_flops,
        12 << 20,
        (normed_1, grad_1, gated_1, cot_all, error_in, error_out, factor_in, factor_out),
        [whole] * 4 + list(merge_specs[1]),
        merged_shapes + [shape((RANK, WIDTH + HEAD), half)],
        [],
    )
    merged_in_0, merged_out_0, left = call(
        first_backward,
        "first_backward",
        8 * dot_flops,
        18 << 20,
        (
            device,
            lengths,
            bias_table[0],
            stamps,
            proj_0,
            normed_0,
            *grad_blocks,
            weight_out[0],
            error_in,
            error_out,
            factor_in,
            factor_out,
            left_1,
        ),
        [scalars] * 3 + [whole] * 12 + list(merge_specs[0]) + [whole],
        merged_shapes + [shape((2 * RANK, WIDTH + HEAD), half)],
        [
            pltpu.VMEM((TOKENS, WIDTH), half),
            pltpu.VMEM((TOKENS, WIDE), half),
            pltpu.VMEM((TOKENS, HEAD), half),
            *attention_scratch,
            *backward_scratch,
        ],
    )
    merged = (merged_in_0, merged_out_0, merged_in_1, merged_out_1)
    basis, right = call(
        basis_right,
        "basis_right",
        dot_flops,
        8 << 20,
        (*sum_rep(left), *merged),
        [whole] * 8,
        [shape((2 * RANK, WIDTH + HEAD), full), shape((2 * RANK, WIDE + WIDTH), half)],
        [],
    )
    outs = call(
        finish,
        "finish",
        dot_flops,
        16 << 20,
        (*sum_rep(right), basis, *merged),
        [whole] * 9,
        [
            shape((2, WIDTH, WIDE), full),
            shape((2, HEAD, WIDTH), full),
            shape((2, RANK, WIDE), full),
            shape((2, RANK, WIDTH), full),
            shape((2, WIDTH, WIDE), full),
            shape((2, HEAD, WIDTH), full),
        ],
        [],
    )
    update_in, update_out, next_in, next_out, error_in_next, error_out_next = outs
    return (
        update_in.reshape(2, 1, WIDTH, WIDE),
        update_out.reshape(2, 1, HEAD, WIDTH),
        next_in.reshape(2, 1, RANK, WIDE),
        next_out.reshape(2, 1, RANK, WIDTH),
        error_in_next.reshape(1, 2, 1, WIDTH, WIDE),
        error_out_next.reshape(1, 2, 1, HEAD, WIDTH),
    )


def solution(mesh):
    placed_in = (
        P(("rep", "tp"), None),
        P(("rep", "tp"), None),
        P(None, None, None, "tp", None),
        P(None, "tp", None, None),
        P(None, "tp", None),
        P("rep"),
        P("rep", None),
        P(None, "tp", None, None),
        P(None, "tp", None, None),
        P("rep", None, "tp", None, None),
        P("rep", None, "tp", None, None),
    )
    return jax.shard_map(
        per_device,
        mesh=mesh,
        in_specs=placed_in,
        out_specs=(
            P(None, "tp", None, None),
            P(None, "tp", None, None),
            P(None, "tp", None, None),
            P(None, "tp", None, None),
            P("rep", None, "tp", None, None),
            P("rep", None, "tp", None, None),
        ),
        check_vma=False,
    )
```

time: 569 us -> 244 us (0.43)
  waiting for transfers between devices: 351 us -> 84.5 us
  matrix products: 111 us -> 0 us
  Pallas kernels: 0 us -> 72.2 us
  other arithmetic: 61.1 us -> 0 us
  starting transfers between devices: 1.01 us -> 53.3 us
  local copies, waits for them, and re-layouts: 22.5 us -> 15.9 us
    psum x3 -> x0, waiting for transfers between devices: 225 us -> none  [the longest x1 77.7 us: compress(): lax.psum(left_in.astype(jnp.bfloat16), 'rep').astype(jnp.float32)]
    dot_general x38 -> x0, matrix products: 109 us -> none  [the longest x2 37.5 us: attend(): jnp.einsum('ihk,jhk->hij', query_part, key_part, preferred_element_type=j...]
    ppermute x0 -> x37, waiting for transfers between devices: none -> 79.7 us  [the longest x9 39.2 us: send_tp(): return lax.ppermute(x, 'tp', [(k, (k - 2 * chips) % 8) for k in range(8)])]
    pallas_call x0 -> x10, Pallas kernels: none -> 72.2 us  [call(): pl.pallas_call(body, name=name, **grid, out_shape=outs, in_specs=in_specs...]
    reduce_scatter x2 -> x0, waiting for transfers between devices: 67.9 us -> none  [scatter_rows(): lax.psum_scatter(term(jnp.int32(0), lax.axis_size('tp') * own_rows).astyp...]
    ppermute x0 -> x37, starting transfers between devices: none -> 53.2 us  [the longest x9 17.1 us: send_tp(): return lax.ppermute(x, 'tp', [(k, (k - 2 * chips) % 8) for k in range(8)])]
    all_gather x4 -> x2, waiting for transfers between devices: 57.1 us -> 4.08 us  [the longest x1 4.08 us: per_device(): mix_all = lax.all_gather(weight_out[0], 'tp', axis=0, tiled=True)]
    another operation x21 -> x0, other arithmetic: 27 us -> none  [the longest x12 14.4 us: orthonormal(): lower = jnp.linalg.cholesky(gram)]
  transfers between devices with their start and end apart: 9 -> 39, of which waited for: 9 -> 22; matrix products, arithmetic and copies ran while one was open for 11% -> 3% of each run, Pallas kernels for 0% -> 6%
where the time goes in v1:
time: 244 us; the launch traced here: 241 us
  waiting for transfers between devices  84.5 us (35%)
  Pallas kernels  72.2 us (30%)
  starting transfers between devices  53.3 us (22%)
  local copies, waits for them, and re-layouts  15.9 us (7%)
  between operations  15.2 us (6%)
    pallas_call x10, Pallas kernels, call(): pl.pallas_call(body, name=name, **grid, out_shape=outs, in_specs=in_specs...  72.2 us
    ppermute x9, waiting for transfers between devices, send_tp(): return lax.ppermute(x, 'tp', [(k, (k - 2 * chips) % 8) for k in range(8)])  39.2 us
    ppermute x9, starting transfers between devices, send_tp(): return lax.ppermute(x, 'tp', [(k, (k - 2 * chips) % 8) for k in range(8)])  17.1 us
    ppermute x6, waiting for transfers between devices, ring_z(): lax.ppermute(x, 'rep', [(k, k - k % 4 + (k - step) % 4) for k in range(16)])  14.9 us
    ppermute x6, waiting for transfers between devices, ring_x(): lax.ppermute(x, 'rep', [(k, (k - 4 * step) % 16) for k in range(16)])  11.5 us
    ppermute x3, waiting for transfers between devices, per_device(): lax.ppermute(sums[chips], 'tp', [(k, (k + 2 * chips) % 8) for k in range(...  11.1 us
    ppermute x6, starting transfers between devices, ring_x(): lax.ppermute(x, 'rep', [(k, (k - 4 * step) % 16) for k in range(16)])  10.9 us
    ppermute x6, starting transfers between devices, ring_z(): lax.ppermute(x, 'rep', [(k, k - k % 4 + (k - step) % 4) for k in range(16)])  10.8 us
  transfers between devices with their start and end apart: 39, of which 22 were waited for; matrix products, arithmetic and copies ran while one was open for 3% of the time, Pallas kernels for 6%

profile of v1, /device:TPU:0, one launch (start us, length us, event | category | flops | bytes accessed | tf_op | source)
XLA Modules:
  0.0 241.1 jit_solution(4755438633123507168)
XLA Ops:
  11.8 2.9 %collective-permute-start.1 = (bf16[128,1024]{1,0:T(8,128)(2,1)}, bf16[128,1024]{1,0:T(8,128)(2,1)S(1)}, u32[]{:S(2)}, u32[]{:S(2)}) collective-permute-start(bf16[128,1024]{1,0:T(8,128)(2,1)} %refs_0_.1), channel_id=1, source_target_pairs={{0,4},{1,5},{2,6},{3,7},{4,0},{5,1},{6,2},{7,3},{8,12},{9,13},{10,... | collective-permute-start | bytes 786440 | tf_op jit(solution)/shard_map/ppermute | solution.py:499
  16.0 3.7 %collective-permute-done.2.refs_3_ = bf16[128,1024]{1,0:T(8,128)(2,1)S(1)} collective-permute-done((bf16[128,1024]{1,0:T(8,128)(2,1)}, bf16[128,1024]{1,0:T(8,128)(2,1)S(1)}, u32[]{:S(2)}, u32[]{:S(2)}) %collective-permute-start.2) | collective-permute-done | bytes 262176 | tf_op jit(solution)/shard_map/ppermute | solution.py:499
  19.7 7.9 %collective-permute-done.1.refs_2_ = bf16[128,1024]{1,0:T(8,128)(2,1)S(1)} collective-permute-done((bf16[128,1024]{1,0:T(8,128)(2,1)}, bf16[128,1024]{1,0:T(8,128)(2,1)S(1)}, u32[]{:S(2)}, u32[]{:S(2)}) %collective-permute-start.1) | collective-permute-done | bytes 262176 | tf_op jit(solution)/shard_map/ppermute | solution.py:499
  35.3 6.8 %first_forward.1 = (bf16[1024,1024]{1,0:T(8,128)(2,1)}, bf16[1024,1024]{1,0:T(8,128)(2,1)}, f32[1024,512]{1,0:T(8,128)}, bf16[1024,128]{1,0:T(8,128)(2,1)}) custom-call(s32[1]{0:T(128)} %bitcast.device_ref, s32[1]{0:T(128)S(6)} %copy.38.length_ref, f32[1,16]{1,0:T(1,128)} %get-tuple-element.80.table_ref, s32[1024,1]{1,0:T(8,128)} %copy.25.stamps_ref, ...), custom_call_target="tpu_custom_call" | custom-call | flops 3221225472 | bytes 12582912 | tf_op jit(solution)/shard_map/first_forward/pallas_call | solution.py:68
  48.3 3.8 %collective-permute-done.9.refs_3_ = bf16[1024,128]{1,0:T(8,128)(2,1)S(1)} collective-permute-done((bf16[1024,128]{1,0:T(8,128)(2,1)}, bf16[1024,128]{1,0:T(8,128)(2,1)S(1)}, u32[]{:S(2)}, u32[]{:S(2)}) %collective-permute-start.9) | collective-permute-done | bytes 262176 | tf_op jit(solution)/shard_map/ppermute | solution.py:499
  52.2 10.6 %collective-permute-done.8.refs_2_ = bf16[1024,128]{1,0:T(8,128)(2,1)S(1)} collective-permute-done((bf16[1024,128]{1,0:T(8,128)(2,1)}, bf16[1024,128]{1,0:T(8,128)(2,1)S(1)}, u32[]{:S(2)}, u32[]{:S(2)}) %collective-permute-start.8) | collective-permute-done | bytes 262176 | tf_op jit(solution)/shard_map/ppermute | solution.py:499
  65.5 4.1 %all-gather.6.cloned.1.call-done = bf16[1,1,1024,1024]{3,2,1,0:T(8,128)(2,1)} async-done(((bf16[1,1,128,1024]{3,2,1,0:T(8,128)(2,1)}), bf16[1,1,1024,1024]{3,2,1,0:T(8,128)(2,1)}) %all-gather.6.cloned.1.call-update) | async-done | bytes 2097168 | tf_op jit(solution)/shard_map/all_gather | solution.py:566
  69.7 19.9 %second_layer.1 = (bf16[1024,1024]{1,0:T(8,128)(2,1)}, bf16[1024,512]{1,0:T(8,128)(2,1)}, bf16[1024,128]{1,0:T(8,128)(2,1)}, bf16[512,1024]{1,0:T(8,128)(2,1)}, ...) custom-call(s32[1]{0:T(128)} %bitcast.device_ref, s32[1]{0:T(128)S(6)} %copy.38.length_ref, ...), custom_call_target="tpu_custom_call" | custom-call | flops 10737418240 | bytes 18874368 | tf_op jit(solution)/shard_map/second_layer/pallas_call | solution.py:68
  101.0 5.6 %collective-permute-done.15.b_ref = bf16[128,1024]{1,0:T(8,128)(2,1)S(1)} collective-permute-done((bf16[128,1024]{1,0:T(8,128)(2,1)}, bf16[128,1024]{1,0:T(8,128)(2,1)S(1)}, u32[]{:S(2)}, u32[]{:S(2)}) %collective-permute-start.15) | collective-permute-done | bytes 262176 | tf_op jit(solution)/shard_map/ppermute | solution.py:645
  106.6 4.9 %collective-permute-done.16.c_ref = bf16[128,1024]{1,0:T(8,128)(2,1)S(1)} collective-permute-done((bf16[128,1024]{1,0:T(8,128)(2,1)}, bf16[128,1024]{1,0:T(8,128)(2,1)S(1)}, u32[]{:S(2)}, u32[]{:S(2)}) %collective-permute-start.16) | collective-permute-done | bytes 262176 | tf_op jit(solution)/shard_map/ppermute | solution.py:645
  120.4 4.4 %collective-permute-done.20.refs_3_ = bf16[128,1024]{1,0:T(8,128)(2,1)S(1)} collective-permute-done((bf16[128,1024]{1,0:T(8,128)(2,1)}, bf16[128,1024]{1,0:T(8,128)(2,1)S(1)}, u32[]{:S(2)}, u32[]{:S(2)}) %collective-permute-start.20) | collective-permute-done | bytes 262176 | tf_op jit(solution)/shard_map/ppermute | solution.py:499
  124.8 6.8 %collective-permute-done.19.refs_2_ = bf16[128,1024]{1,0:T(8,128)(2,1)S(1)} collective-permute-done((bf16[128,1024]{1,0:T(8,128)(2,1)}, bf16[128,1024]{1,0:T(8,128)(2,1)S(1)}, u32[]{:S(2)}, u32[]{:S(2)}) %collective-permute-start.19) | collective-permute-done | bytes 262176 | tf_op jit(solution)/shard_map/ppermute | solution.py:499
  131.6 9.0 %collective-permute-start.22 = (bf16[128,1024]{1,0:T(8,128)(2,1)S(1)}, bf16[128,1024]{1,0:T(8,128)(2,1)S(1)}, u32[]{:S(2)}, u32[]{:S(2)}) collective-permute-start(bf16[128,1024]{1,0:T(8,128)(2,1)S(1)} %collective-permute-done.18.refs_1_), channel_id=1, source_target_pairs={{0,1},{1,0},{2,3},{3,2},{4,5},{5,4},{6,7},{7,6},{8,9},{9,8},{10,11... | collective-permute-start | bytes 786440 | tf_op jit(solution)/shard_map/ppermute | solution.py:503
  140.6 6.5 %second_merge.1 = (f32[1024,512]{1,0:T(8,128)}, f32[128,1024]{1,0:T(8,128)}, bf16[32,1152]{1,0:T(8,128)(2,1)}) custom-call(bf16[1024,1024]{1,0:T(8,128)(2,1)} %get-tuple-element.45.normed_ref, bf16[1024,512]{1,0:T(8,128)(2,1)} %get-tuple-element.46.grad_ref, bf16[1024,128]{1,0:T(8,128)(2,1)} %get-tuple-element.47.gated_ref, ...), custom_call_target="tpu_custom_call" | custom-call | flops 3221225472 | bytes 12582912 | tf_op jit(solution)/shard_map/second_merge/pallas_call | solution.py:68
  148.1 13.3 %first_backward.1 = (f32[1024,512]{1,0:T(8,128)}, f32[128,1024]{1,0:T(8,128)}, bf16[64,1152]{1,0:T(8,128)(2,1)}) custom-call(s32[1]{0:T(128)} %bitcast.device_ref, s32[1]{0:T(128)S(6)} %copy.38.length_ref, f32[1,16]{1,0:T(1,128)} %get-tuple-element.80.table_ref, s32[1024,1]{1,0:T(8,128)} %copy.25.stamps_ref, f32[1024,512]{1,0:T(8,128)} %get-tuple-element.34.proj_ref, ...), custom_call_target="tpu_custom_call" | custom-call | flops 8589934592 | bytes 18874368 | tf_op jit(solution)/shard_map/first_backward/pallas_call | solution.py:68
  163.5 4.3 %collective-permute-start.26 = (bf16[64,1152]{1,0:T(8,128)(2,1)}, bf16[64,1152]{1,0:T(8,128)(2,1)S(1)}, u32[]{:S(2)}, u32[]{:S(2)}) collective-permute-start(bf16[64,1152]{1,0:T(8,128)(2,1)} %get-tuple-element.49.a_ref), channel_id=1, source_target_pairs={{0,16},{8,24},{16,0},{24,8},{32,48},{40,56},{48,32},{56,40},{64,80... | collective-permute-start | bytes 442376 | tf_op jit(solution)/shard_map/ppermute | solution.py:513
  170.9 4.3 %collective-permute-done.26.c_ref = bf16[64,1152]{1,0:T(8,128)(2,1)S(1)} collective-permute-done((bf16[64,1152]{1,0:T(8,128)(2,1)}, bf16[64,1152]{1,0:T(8,128)(2,1)S(1)}, u32[]{:S(2)}, u32[]{:S(2)}) %collective-permute-start.26) | collective-permute-done | bytes 147488 | tf_op jit(solution)/shard_map/ppermute | solution.py:513
  180.0 2.8 %collective-permute-start.29 = (bf16[64,1152]{1,0:T(8,128)(2,1)}, bf16[64,1152]{1,0:T(8,128)(2,1)S(1)}, u32[]{:S(2)}, u32[]{:S(2)}) collective-permute-start(bf16[64,1152]{1,0:T(8,128)(2,1)} %ring_sum.2.refs_0_), channel_id=1, source_target_pairs={{0,64},{8,72},{16,80},{24,88},{32,96},{40,104},{48,112},{56,120},{... | collective-permute-start | bytes 442376 | tf_op jit(solution)/shard_map/ppermute | solution.py:520
  185.6 3.8 %collective-permute-done.29.refs_2_ = bf16[64,1152]{1,0:T(8,128)(2,1)S(1)} collective-permute-done((bf16[64,1152]{1,0:T(8,128)(2,1)}, bf16[64,1152]{1,0:T(8,128)(2,1)S(1)}, u32[]{:S(2)}, u32[]{:S(2)}) %collective-permute-start.29) | collective-permute-done | bytes 147488 | tf_op jit(solution)/shard_map/ppermute | solution.py:520
  190.1 9.0 %basis_right.1 = (f32[64,1152]{1,0:T(8,128)}, bf16[64,1536]{1,0:T(8,128)(2,1)}) custom-call(bf16[64,1152]{1,0:T(8,128)(2,1)} %ring_sum.2.refs_0_, bf16[64,1152]{1,0:T(8,128)(2,1)} %copy-done.12, bf16[64,1152]{1,0:T(8,128)(2,1)} %copy-done.11, bf16[64,1152]{1,0:T(8,128)(2,1)} %copy-done.10, f32[1024,512]{1,0:T(8,128)} %get-tuple-element.50.refs_4_.refs_5_, ...), custom_call_target="tpu_custom_call" | custom-call | flops 1073741824 | bytes 8388608 | tf_op jit(solution)/shard_map/basis_right/pallas_call | solution.py:68
  202.7 4.8 %collective-permute-done.33.d_ref = bf16[64,1536]{1,0:T(8,128)(2,1)S(1)} collective-permute-done((bf16[64,1536]{1,0:T(8,128)(2,1)}, bf16[64,1536]{1,0:T(8,128)(2,1)S(1)}, u32[]{:S(2)}, u32[]{:S(2)}) %collective-permute-start.33) | collective-permute-done | bytes 196640 | tf_op jit(solution)/shard_map/ppermute | solution.py:513
  207.5 3.4 %collective-permute-done.32.c_ref = bf16[64,1536]{1,0:T(8,128)(2,1)S(1)} collective-permute-done((bf16[64,1536]{1,0:T(8,128)(2,1)}, bf16[64,1536]{1,0:T(8,128)(2,1)S(1)}, u32[]{:S(2)}, u32[]{:S(2)}) %collective-permute-start.32) | collective-permute-done | bytes 196640 | tf_op jit(solution)/shard_map/ppermute | solution.py:513
  219.2 4.3 %collective-permute-done.36.refs_3_ = bf16[64,1536]{1,0:T(8,128)(2,1)S(1)} collective-permute-done((bf16[64,1536]{1,0:T(8,128)(2,1)}, bf16[64,1536]{1,0:T(8,128)(2,1)S(1)}, u32[]{:S(2)}, u32[]{:S(2)}) %collective-permute-start.36) | collective-permute-done | bytes 196640 | tf_op jit(solution)/shard_map/ppermute | solution.py:520
  226.4 7.7 %finish.1 = (f32[2,1024,512]{2,1,0:T(8,128)}, f32[2,128,1024]{2,1,0:T(8,128)}, f32[2,32,512]{2,1,0:T(8,128)}, f32[2,32,1024]{2,1,0:T(8,128)}, f32[2,1024,512]{2,1,0:T(8,128)}, /*index=5*/f32[2,128,1024]{2,1,0:T(8,128)}) custom-call(bf16[64,1536]{1,0:T(8,128)(2,1)} %ring_sum.3.refs_0_, bf16[64,1536]{1,0:T(8,128)(2,1)} %copy-done.6, ...), custom_call_target="tpu_custom_call" | custom-call | flops 1073741824 | bytes 16777216 | tf_op jit(solution)/shard_map/finish/pallas_call | solution.py:68
  (146 shorter events, 71.3 us)
Async XLA Ops:
  7.2 58.4 %all-gather.4.cloned.1.call-start = ((), (), s32[]{:S(2)}) async-start(), calls=%async_computation | async-start | bytes 2359296 | tf_op jit(solution)/shard_map/all_gather | solution.py:567
  7.9 61.7 %all-gather.6.cloned.1.call-start = ((), (), s32[]{:S(2)}) async-start(), calls=%async_computation.1 | async-start | bytes 2359296 | tf_op jit(solution)/shard_map/all_gather | solution.py:566
  10.0 9.7 %collective-permute-start.2 = (bf16[128,1024]{1,0:T(8,128)(2,1)}, bf16[128,1024]{1,0:T(8,128)(2,1)S(1)}, u32[]{:S(2)}, u32[]{:S(2)}) collective-permute-start(bf16[128,1024]{1,0:T(8,128)(2,1)} %refs_0_.1), channel_id=1, source_target_pairs={{0,2},{1,3},{2,4},{3,5},{4,6},{5,7},{6,0},{7,1},{8,10},{9,11},{10,... | collective-permute-start | bytes 786440 | tf_op jit(solution)/shard_map/ppermute | solution.py:499
  11.8 15.9 %collective-permute-start.1 = (bf16[128,1024]{1,0:T(8,128)(2,1)}, bf16[128,1024]{1,0:T(8,128)(2,1)S(1)}, u32[]{:S(2)}, u32[]{:S(2)}) collective-permute-start(bf16[128,1024]{1,0:T(8,128)(2,1)} %refs_0_.1), channel_id=1, source_target_pairs={{0,4},{1,5},{2,6},{3,7},{4,0},{5,1},{6,2},{7,3},{8,12},{9,13},{10,... | collective-permute-start | bytes 786440 | tf_op jit(solution)/shard_map/ppermute | solution.py:499
  14.7 14.0 %collective-permute-start = (bf16[128,1024]{1,0:T(8,128)(2,1)}, bf16[128,1024]{1,0:T(8,128)(2,1)S(1)}, u32[]{:S(2)}, u32[]{:S(2)}) collective-permute-start(bf16[128,1024]{1,0:T(8,128)(2,1)} %refs_0_.1), channel_id=1, source_target_pairs={{0,6},{1,7},{2,0},{3,1},{4,2},{5,3},{6,4},{7,5},{8,14},{9,15},{10,... | collective-permute-start | bytes 786440 | tf_op jit(solution)/shard_map/ppermute | solution.py:499
  16.0 18.5 %collective-permute-start.3 = (bf16[128,1024]{1,0:T(8,128)(2,1)}, bf16[128,1024]{1,0:T(8,128)(2,1)S(1)}, u32[]{:S(2)}, u32[]{:S(2)}) collective-permute-start(bf16[128,1024]{1,0:T(8,128)(2,1)} %refs_0_.1), channel_id=1, source_target_pairs={{0,1},{1,0},{2,3},{3,2},{4,5},{5,4},{6,7},{7,6},{8,9},{9,8},{10,11... | collective-permute-start | bytes 786440 | tf_op jit(solution)/shard_map/ppermute | solution.py:503
  19.7 14.8 %collective-permute-start.6 = (bf16[128,1024]{1,0:T(8,128)(2,1)S(1)}, bf16[128,1024]{1,0:T(8,128)(2,1)S(1)}, u32[]{:S(2)}, u32[]{:S(2)}) collective-permute-start(bf16[128,1024]{1,0:T(8,128)(2,1)S(1)} %collective-permute-done.2.refs_3_), channel_id=1, source_target_pairs={{0,1},{1,0},{2,3},{3,2},{4,5},{5,4},{6,7},{7,6},{8,9},{9,8},{10,11... | collective-permute-start | bytes 786440 | tf_op jit(solution)/shard_map/ppermute | solution.py:503
  42.2 10.0 %collective-permute-start.9 = (bf16[1024,128]{1,0:T(8,128)(2,1)}, bf16[1024,128]{1,0:T(8,128)(2,1)S(1)}, u32[]{:S(2)}, u32[]{:S(2)}) collective-permute-start(bf16[1024,128]{1,0:T(8,128)(2,1)} %get-tuple-element.37.refs_0_), channel_id=1, source_target_pairs={{0,2},{1,3},{2,4},{3,5},{4,6},{5,7},{6,0},{7,1},{8,10},{9,11},{10,... | collective-permute-start | bytes 786440 | tf_op jit(solution)/shard_map/ppermute | solution.py:499
  43.7 19.1 %collective-permute-start.8 = (bf16[1024,128]{1,0:T(8,128)(2,1)}, bf16[1024,128]{1,0:T(8,128)(2,1)S(1)}, u32[]{:S(2)}, u32[]{:S(2)}) collective-permute-start(bf16[1024,128]{1,0:T(8,128)(2,1)} %get-tuple-element.37.refs_0_), channel_id=1, source_target_pairs={{0,4},{1,5},{2,6},{3,7},{4,0},{5,1},{6,2},{7,3},{8,12},{9,13},{10,... | collective-permute-start | bytes 786440 | tf_op jit(solution)/shard_map/ppermute | solution.py:499
  46.3 17.5 %collective-permute-start.7 = (bf16[1024,128]{1,0:T(8,128)(2,1)}, bf16[1024,128]{1,0:T(8,128)(2,1)S(1)}, u32[]{:S(2)}, u32[]{:S(2)}) collective-permute-start(bf16[1024,128]{1,0:T(8,128)(2,1)} %get-tuple-element.37.refs_0_), channel_id=1, source_target_pairs={{0,6},{1,7},{2,0},{3,1},{4,2},{5,3},{6,4},{7,5},{8,14},{9,15},{10,... | collective-permute-start | bytes 786440 | tf_op jit(solution)/shard_map/ppermute | solution.py:499
  48.3 16.9 %collective-permute-start.10 = (bf16[1024,128]{1,0:T(8,128)(2,1)}, bf16[1024,128]{1,0:T(8,128)(2,1)S(1)}, u32[]{:S(2)}, u32[]{:S(2)}) collective-permute-start(bf16[1024,128]{1,0:T(8,128)(2,1)} %get-tuple-element.37.refs_0_), channel_id=1, source_target_pairs={{0,1},{1,0},{2,3},{3,2},{4,5},{5,4},{6,7},{7,6},{8,9},{9,8},{10,11... | collective-permute-start | bytes 786440 | tf_op jit(solution)/shard_map/ppermute | solution.py:503
  52.2 13.0 %collective-permute-start.13 = (bf16[1024,128]{1,0:T(8,128)(2,1)S(1)}, bf16[1024,128]{1,0:T(8,128)(2,1)S(1)}, u32[]{:S(2)}, u32[]{:S(2)}) collective-permute-start(bf16[1024,128]{1,0:T(8,128)(2,1)S(1)} %collective-permute-done.9.refs_3_), channel_id=1, source_target_pairs={{0,1},{1,0},{2,3},{3,2},{4,5},{5,4},{6,7},{7,6},{8,9},{9,8},{10,11... | collective-permute-start | bytes 786440 | tf_op jit(solution)/shard_map/ppermute | solution.py:503
  96.0 10.6 %collective-permute-start.15 = (bf16[128,1024]{1,0:T(8,128)(2,1)}, bf16[128,1024]{1,0:T(8,128)(2,1)S(1)}, u32[]{:S(2)}, u32[]{:S(2)}) collective-permute-start(bf16[128,1024]{1,0:T(8,128)(2,1)} %get-tuple-element.41), channel_id=1, source_target_pairs={{0,2},{1,3},{2,4},{3,5},{4,6},{5,7},{6,0},{7,1},{8,10},{9,11},{10,... | collective-permute-start | bytes 786440 | tf_op jit(solution)/shard_map/ppermute | solution.py:645
  97.3 14.2 %collective-permute-start.16 = (bf16[128,1024]{1,0:T(8,128)(2,1)}, bf16[128,1024]{1,0:T(8,128)(2,1)S(1)}, u32[]{:S(2)}, u32[]{:S(2)}) collective-permute-start(bf16[128,1024]{1,0:T(8,128)(2,1)} %get-tuple-element.42), channel_id=1, source_target_pairs={{0,4},{1,5},{2,6},{3,7},{4,0},{5,1},{6,2},{7,3},{8,12},{9,13},{10,... | collective-permute-start | bytes 786440 | tf_op jit(solution)/shard_map/ppermute | solution.py:645
  99.2 12.9 %collective-permute-start.17 = (bf16[128,1024]{1,0:T(8,128)(2,1)}, bf16[128,1024]{1,0:T(8,128)(2,1)S(1)}, u32[]{:S(2)}, u32[]{:S(2)}) collective-permute-start(bf16[128,1024]{1,0:T(8,128)(2,1)} %get-tuple-element.43), channel_id=1, source_target_pairs={{0,6},{1,7},{2,0},{3,1},{4,2},{5,3},{6,4},{7,5},{8,14},{9,15},{10,... | collective-permute-start | bytes 786440 | tf_op jit(solution)/shard_map/ppermute | solution.py:645
  117.1 14.5 %collective-permute-start.19 = (bf16[128,1024]{1,0:T(8,128)(2,1)}, bf16[128,1024]{1,0:T(8,128)(2,1)S(1)}, u32[]{:S(2)}, u32[]{:S(2)}) collective-permute-start(bf16[128,1024]{1,0:T(8,128)(2,1)} %norm_backward.1.refs_0_), channel_id=1, source_target_pairs={{0,4},{1,5},{2,6},{3,7},{4,0},{5,1},{6,2},{7,3},{8,12},{9,13},{10,... | collective-permute-start | bytes 786440 | tf_op jit(solution)/shard_map/ppermute | solution.py:499
  119.5 12.0 %collective-permute-start.18 = (bf16[128,1024]{1,0:T(8,128)(2,1)}, bf16[128,1024]{1,0:T(8,128)(2,1)S(1)}, u32[]{:S(2)}, u32[]{:S(2)}) collective-permute-start(bf16[128,1024]{1,0:T(8,128)(2,1)} %norm_backward.1.refs_0_), channel_id=1, source_target_pairs={{0,6},{1,7},{2,0},{3,1},{4,2},{5,3},{6,4},{7,5},{8,14},{9,15},{10,... | collective-permute-start | bytes 786440 | tf_op jit(solution)/shard_map/ppermute | solution.py:499
  120.4 26.7 %collective-permute-start.21 = (bf16[128,1024]{1,0:T(8,128)(2,1)}, bf16[128,1024]{1,0:T(8,128)(2,1)S(1)}, u32[]{:S(2)}, u32[]{:S(2)}) collective-permute-start(bf16[128,1024]{1,0:T(8,128)(2,1)} %norm_backward.1.refs_0_), channel_id=1, source_target_pairs={{0,1},{1,0},{2,3},{3,2},{4,5},{5,4},{6,7},{7,6},{8,9},{9,8},{10,11... | collective-permute-start | bytes 786440 | tf_op jit(solution)/shard_map/ppermute | solution.py:503
  124.8 22.4 %collective-permute-start.24 = (bf16[128,1024]{1,0:T(8,128)(2,1)S(1)}, bf16[128,1024]{1,0:T(8,128)(2,1)S(1)}, u32[]{:S(2)}, u32[]{:S(2)}) collective-permute-start(bf16[128,1024]{1,0:T(8,128)(2,1)S(1)} %collective-permute-done.20.refs_3_), channel_id=1, source_target_pairs={{0,1},{1,0},{2,3},{3,2},{4,5},{5,4},{6,7},{7,6},{8,9},{9,8},{10,11... | collective-permute-start | bytes 786440 | tf_op jit(solution)/shard_map/ppermute | solution.py:503
  131.6 15.6 %collective-permute-start.23 = (bf16[128,1024]{1,0:T(8,128)(2,1)S(1)}, bf16[128,1024]{1,0:T(8,128)(2,1)S(1)}, u32[]{:S(2)}, u32[]{:S(2)}) collective-permute-start(bf16[128,1024]{1,0:T(8,128)(2,1)S(1)} %collective-permute-done.19.refs_2_), channel_id=1, source_target_pairs={{0,1},{1,0},{2,3},{3,2},{4,5},{5,4},{6,7},{7,6},{8,9},{9,8},{10,11... | collective-permute-start | bytes 786440 | tf_op jit(solution)/shard_map/ppermute | solution.py:503
  131.6 15.6 %collective-permute-start.22 = (bf16[128,1024]{1,0:T(8,128)(2,1)S(1)}, bf16[128,1024]{1,0:T(8,128)(2,1)S(1)}, u32[]{:S(2)}, u32[]{:S(2)}) collective-permute-start(bf16[128,1024]{1,0:T(8,128)(2,1)S(1)} %collective-permute-done.18.refs_1_), channel_id=1, source_target_pairs={{0,1},{1,0},{2,3},{3,2},{4,5},{5,4},{6,7},{7,6},{8,9},{9,8},{10,11... | collective-permute-start | bytes 786440 | tf_op jit(solution)/shard_map/ppermute | solution.py:503
  163.5 11.7 %collective-permute-start.26 = (bf16[64,1152]{1,0:T(8,128)(2,1)}, bf16[64,1152]{1,0:T(8,128)(2,1)S(1)}, u32[]{:S(2)}, u32[]{:S(2)}) collective-permute-start(bf16[64,1152]{1,0:T(8,128)(2,1)} %get-tuple-element.49.a_ref), channel_id=1, source_target_pairs={{0,16},{8,24},{16,0},{24,8},{32,48},{40,56},{48,32},{56,40},{64,80... | collective-permute-start | bytes 442376 | tf_op jit(solution)/shard_map/ppermute | solution.py:513
  200.0 10.8 %collective-permute-start.32 = (bf16[64,1536]{1,0:T(8,128)(2,1)}, bf16[64,1536]{1,0:T(8,128)(2,1)S(1)}, u32[]{:S(2)}, u32[]{:S(2)}) collective-permute-start(bf16[64,1536]{1,0:T(8,128)(2,1)} %get-tuple-element.54.a_ref), channel_id=1, source_target_pairs={{0,16},{8,24},{16,0},{24,8},{32,48},{40,56},{48,32},{56,40},{64,80... | collective-permute-start | bytes 589832 | tf_op jit(solution)/shard_map/ppermute | solution.py:513
  215.9 9.7 %collective-permute-start.35 = (bf16[64,1536]{1,0:T(8,128)(2,1)}, bf16[64,1536]{1,0:T(8,128)(2,1)S(1)}, u32[]{:S(2)}, u32[]{:S(2)}) collective-permute-start(bf16[64,1536]{1,0:T(8,128)(2,1)} %ring_sum.3.refs_0_), channel_id=1, source_target_pairs={{0,64},{8,72},{16,80},{24,88},{32,96},{40,104},{48,112},{56,120},{... | collective-permute-start | bytes 589832 | tf_op jit(solution)/shard_map/ppermute | solution.py:520
  (52 other events, 277.7 us)
Sparse Core Ops, SparseCore 0:
  9.7 28.5 all-gather.3
  40.0 29.6 all-gather.5
